TPU v7x, 32 devices: a whole 2x2x4 slice. The times are simulated.
32 devices in a mesh: groups: 2 (over y), seq: 4 (over z), head: 2 (over x), sub: 2 (over core).
Axes of the slice: x: 2, y: 2, z: 4, core: 2. Of those that a mesh axis runs over, the one named last changes fastest.
Arguments:
- query: bfloat16 [8, 1024, 128], P('head', ('groups', 'seq')), parts along dimension 1, may hold values from -6 to 6
- key: bfloat16 [8, 1024, 128], P('head', ('groups', 'seq')), parts along dimension 1, may hold values from -6 to 6
- value: bfloat16 [8, 128, 1024], P('head', 'sub', ('groups', 'seq')), parts along dimension 2, may hold values from -6 to 6
- beta: float32 [8, 1024], P('head', ('groups', 'seq')), parts along dimension 1, may hold values from 0 to 0.98, as said below
- d_out: bfloat16 [8, 128, 1024], P('head', 'sub', ('groups', 'seq')), parts along dimension 2, may hold values from -6 to 6
Outputs:
- grad_query: float32 [8, 1024, 128], P('head', ('groups', 'seq')), parts along dimension 1
- grad_key: float32 [8, 1024, 128], P('head', ('groups', 'seq')), parts along dimension 1
- grad_value: float32 [8, 128, 1024], P('head', 'sub', ('groups', 'seq')), parts along dimension 2
- grad_beta: float32 [8, 1024], P('head', ('groups', 'seq')), parts along dimension 1
There are 2 independent parts, one for each index of `groups`. A program takes and returns all parts, laid end to end along the dimension named above; each array names one. Nothing has to cross between parts.
Inputs may be any that keep to these rules, and one draw needn't show every extreme that they name: `beta`: every entry is positive.
All inputs are finite; a program needn't handle non-finite values.
Results may differ from a plain program's by a relative error of at most 0.0003.
Values may be sent and summed in bfloat16 or wider, within the bound.
A program may use at most 64 MiB of HBM per device.

v0:
```python
import jax
import jax.numpy as jnp
from jax import lax
from jax.sharding import PartitionSpec as P

CH = 64


EPS = 1e-06
HIGH = lax.Precision.HIGHEST


def passed_along(block, axis, distance):
    devices = range(lax.axis_size(axis))
    route = [(i - distance, i) for i in devices if i - distance in devices]
    return lax.ppermute(block, axis, route)


def carried_in(value, axis, combine, identity):
    count, here = (lax.axis_size(axis), lax.axis_index(axis))
    everything = jax.tree.map(lambda part: lax.all_gather(part, axis), value)
    start = jax.tree.map(
        lambda part, zero: jnp.broadcast_to(jnp.asarray(zero, part.dtype), part.shape),
        value,
        identity,
    )

    def lap(k, before):
        at = count - 1 - k
        reached = at > here
        new = combine(before, jax.tree.map(lambda part: part[at], everything))
        return jax.tree.map(lambda a, b: jnp.where(reached, a, b), new, before)

    return lax.fori_loop(0, count, lap, start)


def block_prep(key_f, beta_arr, value_f, block_len):
    head_count, tokens, key_width = key_f.shape
    value_rows = value_f.shape[1]
    blocks = tokens // block_len
    unit_keys = key_f * lax.rsqrt(jnp.sum(key_f * key_f, -1, keepdims=True) + EPS)
    block_key_rows = unit_keys.reshape(head_count, blocks, block_len, key_width)
    block_vals = jnp.swapaxes(value_f, 1, 2).reshape(head_count, blocks, block_len, value_rows)
    block_beta = beta_arr.reshape(head_count, blocks, block_len)
    inner_keys = jnp.einsum("hnck,hndk->hncd", block_key_rows, block_key_rows, precision=HIGH)
    strictly_lower_mask = jnp.tril(jnp.ones((block_len, block_len), jnp.float32), -1)
    nil_part = -block_beta[..., :, None] * inner_keys * strictly_lower_mask
    identity = jnp.eye(block_len, dtype=jnp.float32)
    inverse = identity + nil_part
    nil_power = nil_part
    for doubling_level in range((block_len - 1).bit_length() - 1):
        nil_power = jnp.einsum("hncd,hnde->hnce", nil_power, nil_power, precision=HIGH)
        inverse = jnp.einsum("hncd,hnde->hnce", inverse, identity + nil_power, precision=HIGH)
    weights = inverse * block_beta[..., None, :]
    w_keys = jnp.einsum("hncd,hndk->hnck", weights, block_key_rows, precision=HIGH)
    w_vals = jnp.einsum("hncd,hndv->hncv", weights, block_vals, precision=HIGH)
    return (block_key_rows, w_keys, w_vals)


def chain_maps(earlier, later):
    trans = jnp.einsum("hij,hjk->hik", earlier[0], later[0], precision=HIGH)
    offset = jnp.einsum("hvj,hjk->hvk", earlier[1], later[0], precision=HIGH) + later[1]
    return (trans, offset)


def chain_adjoint(earlier, later):
    trans = jnp.einsum("hij,hjk->hik", later[0], earlier[0], precision=HIGH)
    offset = jnp.einsum("hvj,hkj->hvk", earlier[1], later[0], precision=HIGH) + later[1]
    return (trans, offset)


def block_maps(block_key_rows, w_keys, w_vals):
    key_width = block_key_rows.shape[-1]
    identity = jnp.eye(key_width, dtype=jnp.float32)
    trans_blocks = identity - jnp.einsum("hnck,hncj->hnkj", w_keys, block_key_rows, precision=HIGH)
    offset_blocks = jnp.einsum("hncv,hnck->hnvk", w_vals, block_key_rows, precision=HIGH)

    def compose(carried, pieces):
        return (chain_maps(carried, pieces), None)

    start = (
        jnp.broadcast_to(identity, trans_blocks[:, 0].shape),
        jnp.zeros_like(offset_blocks[:, 0]),
    )
    result, _ = lax.scan(
        compose, start, (jnp.moveaxis(trans_blocks, 1, 0), jnp.moveaxis(offset_blocks, 1, 0))
    )
    return result


def block_run(query_s, block_key_rows, w_keys, w_vals, entry_state):
    block_len = block_key_rows.shape[2]
    causal = jnp.tril(jnp.ones((block_len, block_len), jnp.float32))

    def advance(memory_state, pieces):
        query_blk, key_blk, wkey_blk, wval_blk = pieces
        new_vals = wval_blk - jnp.einsum("hck,hvk->hcv", wkey_blk, memory_state, precision=HIGH)
        scores = jnp.einsum("hck,hdk->hcd", query_blk, key_blk, precision=HIGH) * causal
        output = jnp.einsum("hck,hvk->hcv", query_blk, memory_state, precision=HIGH)
        output = output + jnp.einsum("hcd,hdv->hcv", scores, new_vals, precision=HIGH)
        memory_state = memory_state + jnp.einsum("hcv,hck->hvk", new_vals, key_blk, precision=HIGH)
        return (memory_state, output)

    pieces = (
        jnp.moveaxis(query_s, 1, 0),
        jnp.moveaxis(block_key_rows, 1, 0),
        jnp.moveaxis(w_keys, 1, 0),
        jnp.moveaxis(w_vals, 1, 0),
    )
    exit_state, outputs = lax.scan(advance, entry_state, pieces)
    return (jnp.moveaxis(outputs, 0, 1), exit_state)


def forward_entry(trans, offset, zero_state):
    chain_len = lax.axis_size("seq")

    def relay(index_step, carried):
        entry_state = passed_along(carried[1], "seq", 1)
        exit_state = jnp.einsum("hvj,hjk->hvk", entry_state, trans, precision=HIGH) + offset
        return (entry_state, exit_state)

    entry_state, _ = lax.fori_loop(0, chain_len - 1, relay, (zero_state, offset))
    return entry_state


def adjoint_exit(trans, entry_grad, eye_state, zero_state):
    _, exit_adjoint = carried_in((trans, entry_grad), "seq", chain_adjoint, (eye_state, zero_state))
    return exit_adjoint


def shards(query, key, value, beta, d_out):
    head_count, tokens, key_width = query.shape
    block_len = CH
    blocks = tokens // block_len
    value_use, grad_use = (value, d_out)
    value_f = value_use.astype(jnp.float32)
    key_f = key.astype(jnp.float32)

    def prep_fn(key_argument, beta_arg, value_arg):
        return block_prep(key_argument, beta_arg, value_arg, block_len)

    (block_key_rows, w_keys, w_vals), prep_back = jax.vjp(prep_fn, key_f, beta, value_f)
    trans, offset = block_maps(block_key_rows, w_keys, w_vals)
    value_rows = value_f.shape[1]
    eye_state = jnp.broadcast_to(
        jnp.eye(key_width, dtype=jnp.float32), (head_count, key_width, key_width)
    )
    zero_state = jnp.zeros((head_count, value_rows, key_width), jnp.float32)
    query_s = query.astype(jnp.float32).reshape(
        head_count, blocks, block_len, key_width
    ) * key_width ** (-0.5)
    out_grad = jnp.swapaxes(grad_use.astype(jnp.float32), 1, 2).reshape(
        head_count, blocks, block_len, value_rows
    )
    _, zero_back = jax.vjp(block_run, query_s, block_key_rows, w_keys, w_vals, zero_state)
    entry_grad = zero_back((out_grad, zero_state))[4]
    exit_adjoint = adjoint_exit(trans, entry_grad, eye_state, zero_state)
    entry_state = forward_entry(trans, offset, zero_state)
    _, run_back = jax.vjp(block_run, query_s, block_key_rows, w_keys, w_vals, entry_state)
    summed = run_back((out_grad, exit_adjoint))
    grad_key, grad_beta, grad_value = prep_back((summed[1], summed[2], summed[3]))
    grad_query = summed[0].reshape(head_count, tokens, key_width) * key_width ** (-0.5)
    grad_query, grad_key, grad_beta = lax.psum((grad_query, grad_key, grad_beta), "sub")
    return (grad_query, grad_key, grad_value, grad_beta)


def solution(mesh):
    placed = (
        P("head", ("groups", "seq"), None),
        P("head", ("groups", "seq"), None),
        P("head", "sub", ("groups", "seq")),
        P("head", ("groups", "seq")),
        P("head", "sub", ("groups", "seq")),
    )
    return jax.shard_map(
        shards,
        mesh=mesh,
        in_specs=placed,
        out_specs=(
            P("head", ("groups", "seq"), None),
            P("head", ("groups", "seq"), None),
            P("head", "sub", ("groups", "seq")),
            P("head", ("groups", "seq")),
        ),
        check_vma=False,
    )
```

profile of v0, /device:TPU:0, one launch (start us, length us, event | category | flops | bytes accessed | tf_op | source)
XLA Modules:
  0.0 158.3 jit_solution(625661656526080149)
XLA Ops:
  7.3 1.1 fusion.118
  19.0 1.0 fusion.116
  20.0 2.1 %while.111 = (s32[]{:T(128)}, f32[4,128,128]{1,2,0:T(8,128)S(1)}, f32[4,64,128]{2,1,0:T(8,128)S(1)}, f32[2,4,128,128]{3,2,0,1:T(8,128)S(1)}, f32[2,4,64,128]{3,2,0,1:T(8,128)S(1)}, /*index=5*/s32[]{:T(128)}, s32[]{:T(128)}) while((s32[]{:T(128)}, f32[4,128,128]{1,2,0:T(8,128)S(1)}, f32[4,64,128]{2,1,0:T(8,128)S(1)}, ...), condition=%wide.region_2.3_spmd.clone, body=%wide.region_1.2_spmd.clone.sunk | while | flops 151060480 | bytes 2229339 | solution.py:85
  23.8 0.9 copy-done.42
  25.8 2.9 %while.112 = (s32[]{:T(128)}, f32[4,64,128]{2,1,0:T(8,128)S(1)}, f32[2,4,64,64]{2,3,1,0:T(8,128)S(1)}, f32[2,4,64,128]{3,2,1,0:T(8,128)S(1)}, f32[2,4,64,128]{3,...) while((s32[]{:T(128)}, f32[4,64,128]{2,1,0:T(8,128)S(1)}, ...), condition=%wide.region_6.7_spmd.clone, body=%wide.region_5.6_spmd.clone.sunk | while | flops 88244224 | bytes 1837691 | solution.py:110
  28.7 25.1 %all-gather.1 = f32[16,64,128]{2,1,0:T(8,128)} all-gather(f32[4,64,128]{2,1,0:T(8,128)S(1)} %get-tuple-element.691), channel_id=3, replica_groups=mesh['groups'=2,'seq'=4,'head'=2,'sub'=2] {'seq'}, dimensions={0}, use_global_device_ids=true | all-gather | bytes 655360 | tf_op jit(solution)/shard_map/all_gather | solution.py:21
  53.8 23.8 %while.107 = (s32[]{:T(128)}, f32[4,64,128]{2,1,0:T(8,128)}, f32[4,64,128]{2,1,0:T(8,128)S(1)}, f32[4,128,128]{2,1,0:T(8,128)S(1)}, f32[4,64,128]{2,1,0:T(8,128)S(1)}, /*index=5*/s32[]{:T(128)}) while((s32[]{:T(128)}, f32[4,64,128]{2,1,0:T(8,128)}, f32[4,64,128]{2,1,0:T(8,128)S(1)}, f32[4,128,128]{2,1,0:T(8,128)S(1)}, ...), condition=%wide.region_10.11_spmd, body=%wide.region_9.10_spmd.sunk | while | flops 50364416 | bytes 1704073 | solution.py:122
  53.8 2.3 %collective-permute-start = (f32[4,64,128]{2,1,0:T(8,128)S(1)}, f32[4,64,128]{2,1,0:T(8,128)S(1)}, u32[]{:S(2)}, u32[]{:S(2)}) collective-permute-start(f32[4,64,128]{2,1,0:T(8,128)S(1)} %get-tuple-element.1450), channel_id=1, source_target_pairs={{0,4},{4,8},{8,12},{1,5},{5,9},{9,13},{2,6},{6,10},{10,14},{3,7},{... | collective-permute-start | bytes 393224 | tf_op jit(solution)/shard_map/while/body/eval_jaxpr/ppermute | solution.py:16
  56.1 5.8 %collective-permute-done = f32[4,64,128]{2,1,0:T(8,128)S(1)} collective-permute-done((f32[4,64,128]{2,1,0:T(8,128)S(1)}, f32[4,64,128]{2,1,0:T(8,128)S(1)}, u32[]{:S(2)}, u32[]{:S(2)}) %collective-permute-start) | collective-permute-done | bytes 131104 | tf_op jit(solution)/shard_map/while/body/eval_jaxpr/ppermute | solution.py:16
  62.6 4.4 %collective-permute-start = (f32[4,64,128]{2,1,0:T(8,128)S(1)}, f32[4,64,128]{2,1,0:T(8,128)S(1)}, u32[]{:S(2)}, u32[]{:S(2)}) collective-permute-start(f32[4,64,128]{2,1,0:T(8,128)S(1)} %get-tuple-element.1450), channel_id=1, source_target_pairs={{0,4},{4,8},{8,12},{1,5},{5,9},{9,13},{2,6},{6,10},{10,14},{3,7},{... | collective-permute-start | bytes 393224 | tf_op jit(solution)/shard_map/while/body/eval_jaxpr/ppermute | solution.py:16
  67.0 2.5 %collective-permute-done = f32[4,64,128]{2,1,0:T(8,128)S(1)} collective-permute-done((f32[4,64,128]{2,1,0:T(8,128)S(1)}, f32[4,64,128]{2,1,0:T(8,128)S(1)}, u32[]{:S(2)}, u32[]{:S(2)}) %collective-permute-start) | collective-permute-done | bytes 131104 | tf_op jit(solution)/shard_map/while/body/eval_jaxpr/ppermute | solution.py:16
  70.1 4.3 %collective-permute-start = (f32[4,64,128]{2,1,0:T(8,128)S(1)}, f32[4,64,128]{2,1,0:T(8,128)S(1)}, u32[]{:S(2)}, u32[]{:S(2)}) collective-permute-start(f32[4,64,128]{2,1,0:T(8,128)S(1)} %get-tuple-element.1450), channel_id=1, source_target_pairs={{0,4},{4,8},{8,12},{1,5},{5,9},{9,13},{2,6},{6,10},{10,14},{3,7},{... | collective-permute-start | bytes 393224 | tf_op jit(solution)/shard_map/while/body/eval_jaxpr/ppermute | solution.py:16
  74.5 2.5 %collective-permute-done = f32[4,64,128]{2,1,0:T(8,128)S(1)} collective-permute-done((f32[4,64,128]{2,1,0:T(8,128)S(1)}, f32[4,64,128]{2,1,0:T(8,128)S(1)}, u32[]{:S(2)}, u32[]{:S(2)}) %collective-permute-start) | collective-permute-done | bytes 131104 | tf_op jit(solution)/shard_map/while/body/eval_jaxpr/ppermute | solution.py:16
  78.4 0.9 copy-done.1
  79.3 5.4 %while.109 = (s32[]{:T(128)}, f32[4,64,128]{2,1,0:T(8,128)S(1)}, f32[2,4,64,128]{3,2,1,0:T(8,128)S(1)}, f32[2,4,64,64]{3,2,1,0:T(8,128)S(1)}, f32[2,4,64,64]{3,2...) while((s32[]{:T(128)}, f32[4,64,128]{2,1,0:T(8,128)S(1)}, ...), condition=%wide.region_12.13_spmd.clone, body=%wide.region_11.12_spmd.clone.sunk | while | flops 75571200 | bytes 1886829 | solution.py:110
  79.3 1.2 bitcast_dynamic-update-slice_fusion.6
  81.0 1.0 fusion.330
  82.0 1.2 bitcast_dynamic-update-slice_fusion.6
  83.6 1.0 fusion.330
  84.6 6.5 %while.113 = (s32[]{:T(128)}, f32[4,64,128]{2,1,0:T(8,128)S(1)}, s32[]{:T(128)}, f32[4,4,128,128]{3,2,1,0:T(8,128)}, f32[4,4,64,128]{3,2,1,0:T(8,128)}, /*index=5*/s32[]{:T(128)}, s32[]{:T(128)}, s32[]{:T(128)}, s32[]{:T(128)}) while((s32[]{:T(128)}, f32[4,64,128]{2,1,0:T(8,128)S(1)}, s32[]{:T(128)}, f32[4,4,128,128]{3,2,1,0:T(8,128)}, ...), condition=%wide.region_8.9_spmd.clone, body=%wide.region_7.8_spmd.clone.sunk | while | flops 50462728 | bytes 1051293 | solution.py:34
  84.6 1.6 %fusion.372 = f32[4,64,128]{2,1,0:T(8,128)S(1)} fusion(f32[4,4,128,128]{3,2,1,0:T(8,128)} %get-tuple-element.1436, s32[]{:T(128)S(6)} %select_n.93, f32[4,64,128]{2,1,0:T(8,128)S(1)} %copy.359, f32[4,4,64,128]{3,2,1,0:T(8,128)} %get-tuple-element.1437, pred[]{:T(512)S(6)} %compare.11, pred[]{:T(512)S(6)} %gt.12), kind=kOutput, calls=%fused_computation.132.clone.1 | convolution fusion | flops 50462720 | bytes 788992 | tf_op jit(solution)/shard_map/while/body/eval_jaxpr/hvj,hkj->hvk/dot_general | solution.py:68
  86.3 1.6 %fusion.372 = f32[4,64,128]{2,1,0:T(8,128)S(1)} fusion(f32[4,4,128,128]{3,2,1,0:T(8,128)} %get-tuple-element.1436, s32[]{:T(128)S(6)} %select_n.93, f32[4,64,128]{2,1,0:T(8,128)S(1)} %copy.359, f32[4,4,64,128]{3,2,1,0:T(8,128)} %get-tuple-element.1437, pred[]{:T(512)S(6)} %compare.11, pred[]{:T(512)S(6)} %gt.12), kind=kOutput, calls=%fused_computation.132.clone.1 | convolution fusion | flops 50462720 | bytes 788992 | tf_op jit(solution)/shard_map/while/body/eval_jaxpr/hvj,hkj->hvk/dot_general | solution.py:68
  87.9 1.6 %fusion.372 = f32[4,64,128]{2,1,0:T(8,128)S(1)} fusion(f32[4,4,128,128]{3,2,1,0:T(8,128)} %get-tuple-element.1436, s32[]{:T(128)S(6)} %select_n.93, f32[4,64,128]{2,1,0:T(8,128)S(1)} %copy.359, f32[4,4,64,128]{3,2,1,0:T(8,128)} %get-tuple-element.1437, pred[]{:T(512)S(6)} %compare.11, pred[]{:T(512)S(6)} %gt.12), kind=kOutput, calls=%fused_computation.132.clone.1 | convolution fusion | flops 50462720 | bytes 788992 | tf_op jit(solution)/shard_map/while/body/eval_jaxpr/hvj,hkj->hvk/dot_general | solution.py:68
  89.6 1.6 %fusion.372 = f32[4,64,128]{2,1,0:T(8,128)S(1)} fusion(f32[4,4,128,128]{3,2,1,0:T(8,128)} %get-tuple-element.1436, s32[]{:T(128)S(6)} %select_n.93, f32[4,64,128]{2,1,0:T(8,128)S(1)} %copy.359, f32[4,4,64,128]{3,2,1,0:T(8,128)} %get-tuple-element.1437, pred[]{:T(512)S(6)} %compare.11, pred[]{:T(512)S(6)} %gt.12), kind=kOutput, calls=%fused_computation.132.clone.1 | convolution fusion | flops 50462720 | bytes 788992 | tf_op jit(solution)/shard_map/while/body/eval_jaxpr/hvj,hkj->hvk/dot_general | solution.py:68
  93.4 13.7 %while.110 = (s32[]{:T(128)}, f32[4,64,128]{2,1,0:T(8,128)S(1)}, f32[2,4,64,128]{3,2,1,0:T(8,128)}, f32[2,4,64,128]{3,2,0,1:T(8,128)}, f32[2,4,64,128]{3,2,1,0:T...) while((s32[]{:T(128)}, f32[4,64,128]{2,1,0:T(8,128)S(1)}, ...), condition=%wide.region_14.15_spmd.clone, body=%wide.region_13.14_spmd.clone.sunk | while | flops 226697216 | bytes 10936133 | solution.py:110
  93.7 1.3 bitcast_dynamic-update-slice_fusion.8
  100.6 1.3 bitcast_dynamic-update-slice_fusion.8
  107.1 1.3 fusion.122
  127.0 0.9 add_add_fusion
  130.1 3.0 %psum.23 = f32[4,128]{1,0:T(4,128)} all-reduce(f32[4,128]{1,0:T(4,128)S(1)} %add_any.144), channel_id=1, replica_groups=mesh['groups'=2,'seq'=4,'head'=2,'sub'=2] {'sub'}, use_global_device_ids=true, to_apply=%region_20.21 | all-reduce | flops 512 | bytes 4096 | tf_op jit(solution)/shard_map/psum | solution.py:163
  133.2 15.9 %all-reduce.3.cloned.1.call-done = (f32[4,128,128]{2,1,0:T(8,128)}, f32[4,128,128]{2,1,0:T(8,128)}) async-done(((f32[4,128,128]{2,1,0:T(8,128)}, f32[4,128,128]{2,1,0:T(8,128)}), (f32[4,128,128]{2,1,0:T(8,128)}, f32[4,128,128]{2,1,0:T(8,128)})) %all-reduce.3.cloned.1.call-update) | async-done | bytes 524304 | tf_op jit(solution)/shard_map/psum | solution.py:163
  149.1 1.7 %copy.360 = f32[4,128,128]{2,1,0:T(8,128)} copy(f32[4,128,128]{2,1,0:T(8,128)} %get-tuple-element.1532) | data formatting | bytes 524288
  (250 shorter events, 56.4 us)
Async XLA Ops:
  7.2 1.2 copy-start.29
  7.2 77.5 %all-gather.4.cloned.1.call-start = ((), (), s32[]{:S(2)}) async-start(), calls=%async_computation | async-start | bytes 1310720 | tf_op jit(solution)/shard_map/all_gather | solution.py:21
  7.2 8.6 %copy-start.6 = (f32[64,64]{0,1:T(8,128)}, f32[64,64]{0,1:T(8,128)S(1)}, u32[]{:S(2)}) copy-start(f32[64,64]{0,1:T(8,128)S(1)} %fusion.185) | copy-start | bytes 49156
  9.3 3.7 %copy-start.31 = (f32[64,64]{0,1:T(8,128)}, f32[64,64]{0,1:T(8,128)S(1)}, u32[]{:S(2)}) copy-start(f32[64,64]{0,1:T(8,128)S(1)} %fusion.186) | copy-start | bytes 49156
  10.0 2.9 %copy-start.12 = (f32[4,2,64,64]{2,3,1,0:T(8,128)}, f32[4,2,64,64]{2,3,1,0:T(8,128)S(1)}, u32[]{:S(2)}) copy-start(f32[4,2,64,64]{2,3,1,0:T(8,128)S(1)} %copy.152) | copy-start | bytes 393220
  10.6 3.5 %copy-start.14 = (f32[4,2,64,64]{2,3,1,0:T(8,128)}, f32[4,2,64,64]{2,3,1,0:T(8,128)S(1)}, u32[]{:S(2)}) copy-start(f32[4,2,64,64]{2,3,1,0:T(8,128)S(1)} %copy.155) | copy-start | bytes 393220
  11.1 3.5 %copy-start.16 = (f32[4,2,64,64]{2,3,1,0:T(8,128)}, f32[4,2,64,64]{2,3,1,0:T(8,128)S(1)}, u32[]{:S(2)}) copy-start(f32[4,2,64,64]{2,3,1,0:T(8,128)S(1)} %copy.157) | copy-start | bytes 393220
  12.3 3.6 %copy-start.18 = (f32[4,2,64,64]{2,3,1,0:T(8,128)}, f32[4,2,64,64]{2,3,1,0:T(8,128)S(1)}, u32[]{:S(2)}) copy-start(f32[4,2,64,64]{2,3,1,0:T(8,128)S(1)} %copy.159) | copy-start | bytes 393220
  13.0 3.5 %copy-start.8 = (f32[4,2,64,64]{2,3,1,0:T(8,128)}, f32[4,2,64,64]{2,3,1,0:T(8,128)S(1)}, u32[]{:S(2)}) copy-start(f32[4,2,64,64]{2,3,1,0:T(8,128)S(1)} %convolution_add_fusion.24) | copy-start | bytes 393220
  13.6 1.0 copy-start.20
  14.0 3.7 %copy-start.33 = (bf16[4,128,64]{2,1,0:T(8,128)(2,1)}, bf16[4,128,64]{2,1,0:T(8,128)(2,1)S(1)}, u32[]{:S(2)}) copy-start(bf16[4,128,64]{2,1,0:T(8,128)(2,1)S(1)} %copy.250) | copy-start | bytes 196612
  23.0 126.1 %all-reduce.3.cloned.1.call-start = ((), (), s32[]{:S(2)}) async-start(), calls=%async_computation.1 | async-start | bytes 1048576 | tf_op jit(solution)/shard_map/psum | solution.py:163
  28.7 25.1 %copy-start.2 = (f32[4,128,128]{2,1,0:T(8,128)S(1)}, f32[4,128,128]{2,1,0:T(8,128)}, u32[]{:S(2)}) copy-start(f32[4,128,128]{2,1,0:T(8,128)} %copy.167) | copy-start | bytes 786436
  28.7 25.1 %copy-start.43 = (f32[4,64,128]{2,1,0:T(8,128)S(1)}, f32[4,64,128]{2,1,0:T(8,128)}, u32[]{:S(2)}) copy-start(f32[4,64,128]{2,1,0:T(8,128)} %copy.310) | copy-start | bytes 393220
  53.8 8.1 %collective-permute-start = (f32[4,64,128]{2,1,0:T(8,128)S(1)}, f32[4,64,128]{2,1,0:T(8,128)S(1)}, u32[]{:S(2)}, u32[]{:S(2)}) collective-permute-start(f32[4,64,128]{2,1,0:T(8,128)S(1)} %get-tuple-element.1450), channel_id=1, source_target_pairs={{0,4},{4,8},{8,12},{1,5},{5,9},{9,13},{2,6},{6,10},{10,14},{3,7},{... | collective-permute-start | bytes 393224 | tf_op jit(solution)/shard_map/while/body/eval_jaxpr/ppermute | solution.py:16
  62.6 6.9 %collective-permute-start = (f32[4,64,128]{2,1,0:T(8,128)S(1)}, f32[4,64,128]{2,1,0:T(8,128)S(1)}, u32[]{:S(2)}, u32[]{:S(2)}) collective-permute-start(f32[4,64,128]{2,1,0:T(8,128)S(1)} %get-tuple-element.1450), channel_id=1, source_target_pairs={{0,4},{4,8},{8,12},{1,5},{5,9},{9,13},{2,6},{6,10},{10,14},{3,7},{... | collective-permute-start | bytes 393224 | tf_op jit(solution)/shard_map/while/body/eval_jaxpr/ppermute | solution.py:16
  70.1 6.8 %collective-permute-start = (f32[4,64,128]{2,1,0:T(8,128)S(1)}, f32[4,64,128]{2,1,0:T(8,128)S(1)}, u32[]{:S(2)}, u32[]{:S(2)}) collective-permute-start(f32[4,64,128]{2,1,0:T(8,128)S(1)} %get-tuple-element.1450), channel_id=1, source_target_pairs={{0,4},{4,8},{8,12},{1,5},{5,9},{9,13},{2,6},{6,10},{10,14},{3,7},{... | collective-permute-start | bytes 393224 | tf_op jit(solution)/shard_map/while/body/eval_jaxpr/ppermute | solution.py:16
  95.6 1.0 copy-start.26
  97.2 1.0 copy-start.34
  98.4 1.1 copy-start.35
  102.4 1.0 copy-start.26
  104.1 1.0 copy-start.34
  105.3 1.1 copy-start.35
  107.1 1.3 copy-start.28
  108.4 1.0 copy-start.11
  111.9 1.0 copy-start.19
  115.0 1.0 copy-start.17
  118.1 1.0 copy-start.15
  121.2 1.0 copy-start.13
  123.9 1.0 copy-start.39
  126.9 1.0 copy-start.36
  149.1 1.7 %copy-start.41 = (f32[4,128,128]{2,1,0:T(8,128)S(1)}, f32[4,128,128]{2,1,0:T(8,128)}, u32[]{:S(2)}) copy-start(f32[4,128,128]{2,1,0:T(8,128)} %get-tuple-element.1533) | copy-start | bytes 786436
  (28 other events, 23.0 us)
Sparse Core Ops, SparseCore 0:
  23.1 38.9 all-gather.3
  128.8 20.2 all-reduce.2
where the time goes:
time: 160 us; the launch traced here: 158 us
  matrix products  49.3 us (31%)
  blocking collectives  28.1 us (18%)
  waiting for transfers between devices  26.7 us (17%)
  local copies, waits for them, and re-layouts  24.3 us (15%)
  between operations  14.9 us (9%)
  starting transfers between devices  11.1 us (7%)
  other arithmetic  3.1 us (2%)
    all_gather x1, blocking collectives, carried_in(): everything = jax.tree.map(lambda part: lax.all_gather(part, axis), value)  25.1 us
    psum x1, waiting for transfers between devices, shards(): lax.psum((grad_query, grad_key, grad_beta), 'sub')  15.9 us
    unnamed x86, local copies, waits for them, and re-layouts  12 us
    ppermute x3, starting transfers between devices, passed_along(): return lax.ppermute(block, axis, route)  11 us
    ppermute x3, waiting for transfers between devices, passed_along(): return lax.ppermute(block, axis, route)  10.8 us
    dot_general x15, matrix products, block_prep(): jnp.einsum('hncd,hnde->hnce', nil_power, nil_power, precision=HIGH)  8.18 us
    dot_general x15, matrix products, block_prep(): jnp.einsum('hncd,hnde->hnce', inverse, identity + nil_power, precision=HIGH)  7.77 us
    dot_general x4, matrix products, chain_adjoint(): jnp.einsum('hvj,hkj->hvk', earlier[1], later[0], precision=HIGH) + later[1]  6.35 us
  transfers between devices with their start and end apart: 5, of which 4 were waited for; matrix products, arithmetic and copies ran while one was open for 8% of the time, Pallas kernels for 0%

commit v1 on v0

v1 whole, which is shorter than its diff:
```python
import functools

import jax
import jax.numpy as jnp
from jax import lax
from jax.experimental import pallas as pl
from jax.experimental.pallas import tpu as pltpu
from jax.sharding import PartitionSpec as P

EPS = 1e-06
BASE = 16
F32 = jnp.float32
BF16 = jnp.bfloat16
MESH = pl.DeviceIdType.MESH


def split(x):
    hi = x.astype(BF16)
    return hi, (x - hi.astype(F32)).astype(BF16)


def nn(lhs, rhs):
    a = lhs[0] if len(lhs) == 1 else jnp.concatenate(lhs, axis=1)
    b = rhs[0] if len(rhs) == 1 else jnp.concatenate(rhs, axis=0)
    return jnp.dot(a, b, preferred_element_type=F32)


def nt(lhs, rhs):
    a = lhs[0] if len(lhs) == 1 else jnp.concatenate(lhs, axis=1)
    b = rhs[0] if len(rhs) == 1 else jnp.concatenate(rhs, axis=1)
    return lax.dot_general(a, b, (((1,), (1,)), ((), ())), preferred_element_type=F32)


def left3(s):
    return [s[0], s[0], s[1]]


def right3(s):
    return [s[0], s[1], s[0]]


def nn3(a, b):
    return nn(left3(a), right3(b))


def nt3(a, b):
    return nt(left3(a), right3(b))


def inverses(mats, row, col):
    size = mats[0].shape[0]
    heads = range(len(mats))
    eye = (row == col).astype(F32)
    near = (row // BASE) == (col // BASE)
    power = [split(jnp.where(near, -a, 0.0)) for a in mats]
    inv = [eye + jnp.where(near, -a, 0.0) for a in mats]
    reach = 2
    while reach < BASE:
        power = [split(nn3(p, p)) for p in power]
        inv = [inv[h] + nn3(split(inv[h]), power[h]) for h in heads]
        reach *= 2
    width = BASE
    while width < size:
        pair = ((row // (2 * width)) == (col // (2 * width))) & ((row // width) != (col // width))
        off = [split(jnp.where(pair, a, 0.0)) for a in mats]
        cut = [split(i) for i in inv]
        mid = [split(nn3(off[h], cut[h])) for h in heads]
        inv = [inv[h] - nn3(cut[h], mid[h]) for h in heads]
        width *= 2
    return inv


def kernel(
    n, q_ref, k_ref, v_ref, b_ref, g_ref, gq_ref, gk_ref, gv_ref, gb_ref,
    vin, gin, s_in, s_out, d_in, d_out, dt_s, xt_s, dm_s, gt_s, gvx, gbx,
    in_send, in_recv, f_send, f_recv, r_send, r_recv, o_send, o_recv,
):
    heads, toks, width = q_ref.shape
    mine = heads // 2
    half = v_ref.shape[1]
    idx = lax.axis_index("seq")
    sub = lax.axis_index("sub")
    other = 1 - sub
    right, left = lax.rem(idx + 1, n), lax.rem(idx + n - 1, n)
    scale = width ** (-0.5)
    base = sub * mine
    hs = range(mine)

    barrier = pltpu.get_barrier_semaphore()
    for target in ({"sub": other}, {"seq": right}, {"seq": left}):
        pl.semaphore_signal(barrier, inc=1, device_id=target, device_id_type=MESH)

    def remote(src, dst, send, recv, target):
        return pltpu.make_async_remote_copy(
            src_ref=src, dst_ref=dst, send_sem=send, recv_sem=recv,
            device_id=target, device_id_type=MESH,
        )

    away = pl.ds(other * mine, mine)
    v_copy = remote(v_ref.at[away], vin, in_send.at[0], in_recv.at[0], {"sub": other})
    g_copy = remote(g_ref.at[away], gin, in_send.at[1], in_recv.at[1], {"sub": other})

    def f_copy(h):
        return remote(s_out.at[h], s_in.at[h], f_send.at[h], f_recv.at[h], {"seq": right})

    def r_copy(h):
        return remote(d_out.at[h], d_in.at[h], r_send.at[h], r_recv.at[h], {"seq": left})

    def q_copy(h):
        at = gq_ref.at[base + h]
        return remote(at, at, o_send.at[0, h], o_recv.at[0, h], {"sub": other})

    def k_copy(h):
        at = gk_ref.at[base + h]
        return remote(at, at, o_send.at[1, h], o_recv.at[1, h], {"sub": other})

    def gv_copy(h):
        return remote(
            gvx.at[h], gv_ref.at[base + h], o_send.at[2, h], o_recv.at[2, h], {"sub": other}
        )

    gb_copy = remote(gbx.at[sub], gbx.at[sub], o_send.at[3, 0], o_recv.at[3, 0], {"sub": other})

    pl.semaphore_wait(barrier, 3)
    v_copy.start()
    g_copy.start()

    @pl.when(idx == 0)
    def _():
        s_in[...] = jnp.zeros_like(s_in)

    @pl.when(idx == n - 1)
    def _():
        d_in[...] = jnp.zeros_like(d_in)

    row = lax.broadcasted_iota(jnp.int32, (toks, toks), 0)
    col = lax.broadcasted_iota(jnp.int32, (toks, toks), 1)
    below, lower, above = row > col, row >= col, row < col
    eye = (row == col).astype(F32)

    kb = [k_ref[base + h] for h in hs]
    qb = [q_ref[base + h] for h in hs]
    kf = [k.astype(F32) for k in kb]
    r_col = [lax.rsqrt(jnp.sum(k * k, axis=1, keepdims=True) + EPS) for k in kf]
    r_row = [jnp.broadcast_to(r, (toks, toks)).T for r in r_col]
    b_row = [b_ref[pl.ds(base + h, 1), :] for h in hs]
    b_col = [jnp.broadcast_to(b, (toks, toks)).T for b in b_row]
    both = [nt([kb[h]], [kb[h]]) * r_col[h] * r_row[h] for h in hs]
    tri = inverses([jnp.where(below, b_col[h] * both[h], 0.0) for h in hs], row, col)
    kbt = [k.T for k in kb]
    tri_b = [split(tri[h] * b_row[h]) for h in hs]
    tri_br = [split(tri[h] * (b_row[h] * r_row[h])) for h in hs]
    w_t = [nt([kbt[h]] * 2, list(tri_br[h])) for h in hs]
    trans = [split(eye - nn(list(split(w_t[h] * r_row[h])), [kb[h]] * 2)) for h in hs]
    w_s = [split(w) for w in w_t]

    v_copy.wait_recv()
    g_copy.wait_recv()
    vt = [jnp.concatenate([v_ref[base + h], vin[h]], axis=0) for h in hs]
    gt = [jnp.concatenate([g_ref[base + h], gin[h]], axis=0) for h in hs]
    u_t = [nt([vt[h]] * 2, list(tri_b[h])) for h in hs]
    carry = [nn(list(split(u_t[h] * r_row[h])), [kb[h]] * 2) for h in hs]

    @pl.when(idx == 0)
    def _():
        for h in hs:
            s_out[h] = carry[h]
            f_copy(h).start()

    scores = [
        split(jnp.where(lower, nt([qb[h]], [kb[h]]) * (r_row[h] * scale), 0.0)) for h in hs
    ]
    dd0 = [split(nn([gt[h]] * 2, list(scores[h]))) for h in hs]
    tri_s = [split(t) for t in tri]
    g0 = [nn3(dd0[h], tri_s[h]) for h in hs]
    back = [
        nn([gt[h]], [qb[h]]) * scale
        - nn(list(split(g0[h] * (b_row[h] * r_row[h]))), [kb[h]] * 2)
        for h in hs
    ]

    @pl.when(idx == n - 1)
    def _():
        for h in hs:
            d_out[h] = back[h]
            r_copy(h).start()

    z_t = [
        split(nn([kbt[h]] * 2, list(split(tri[h] * r_col[h])))) for h in hs
    ]
    g_tok = [g.T for g in gt]

    def phase_f():
        for h in hs:

            @pl.when(idx > 0)
            def _():
                f_copy(h).wait_recv()

            @pl.when((idx > 0) & (idx < n - 1))
            def _():
                s_out[h] = nn3(split(s_in[h]), trans[h]) + carry[h]
                f_copy(h).start()

        for h in hs:
            state = split(s_in[h])
            d_t = u_t[h] - nn3(state, w_s[h])
            xt_s[h] = vt[h].astype(F32) - nt(list(state), [kb[h]] * 2) * r_row[h]
            dt_s[h] = d_t
            dm = jnp.where(lower, nn([g_tok[h]] * 2, list(split(d_t))), 0.0)
            dm_s[h] = dm.T * scale
            gq_ref[base + h] = scale * nn(
                [g_tok[h]] * 2 + list(split(dm * r_row[h])), list(state) + [kb[h]] * 2
            )
            q_copy(h).start()

    def phase_r():
        for h in hs:

            @pl.when(idx < n - 1)
            def _():
                r_copy(h).wait_recv()

            @pl.when((idx > 0) & (idx < n - 1))
            def _():
                d_out[h] = nt3(split(d_in[h]), trans[h]) + back[h]
                r_copy(h).start()

        for h in hs:
            g_full = g0[h] + nn3(split(d_in[h]), z_t[h])
            gt_s[h] = g_full
            e_t = g_full * b_row[h]
            gv_ref[base + h] = e_t[:half]
            gvx[h] = e_t[half:]
            gv_copy(h).start()

    pl.when(2 * idx < n)(phase_f)
    phase_r()
    pl.when(2 * idx >= n)(phase_f)

    for h in hs:
        g_full, d_t = gt_s[h], dt_s[h]
        d_tok = split(d_t.T)
        e_tok = split(-(g_full * b_row[h]).T)
        n_un = jnp.where(above, nn3(d_tok, split(g_full)), 0.0)
        gbx[sub, pl.ds(h, 1), :] = jnp.sum(g_full * xt_s[h], axis=0, keepdims=True) - jnp.sum(
            n_un * both[h], axis=0, keepdims=True
        )
        n_t = n_un * -b_row[h]
        sym = split((n_t + n_t.T) * r_row[h])
        d_unit = nn(
            left3(e_tok) + left3(d_tok) + list(sym) + list(split(dm_s[h])),
            right3(split(s_in[h])) + right3(split(d_in[h])) + [kb[h]] * 2 + [qb[h]] * 2,
        )
        unit = kf[h] * r_col[h]
        gk_ref[base + h] = r_col[h] * (
            d_unit - unit * jnp.sum(d_unit * unit, axis=1, keepdims=True)
        )
        k_copy(h).start()
    gb_copy.start()

    v_copy.wait_send()
    g_copy.wait_send()

    @pl.when(idx < n - 1)
    def _():
        for h in hs:
            f_copy(h).wait_send()

    @pl.when(idx > 0)
    def _():
        for h in hs:
            r_copy(h).wait_send()

    for h in hs:
        q_copy(h).wait()
        gv_copy(h).wait()
        k_copy(h).wait()
    gb_copy.wait()
    for s in range(2):
        gb_ref[s * mine : (s + 1) * mine, :] = gbx[s, :mine, :]


def solution(mesh):
    n = mesh.shape["seq"]

    def shards(query, key, value, beta, d_out):
        heads, toks, width = query.shape
        mine, half = heads // 2, value.shape[1]
        full = 2 * half
        vm = pl.BlockSpec(memory_space=pltpu.VMEM)
        dma = pltpu.SemaphoreType.DMA
        square = pltpu.VMEM((mine, full, width), F32)
        by_tok = pltpu.VMEM((mine, full, toks), F32)
        return pl.pallas_call(
            functools.partial(kernel, n),
            out_shape=(
                jax.ShapeDtypeStruct(query.shape, F32),
                jax.ShapeDtypeStruct(key.shape, F32),
                jax.ShapeDtypeStruct(value.shape, F32),
                jax.ShapeDtypeStruct(beta.shape, F32),
            ),
            in_specs=[vm] * 5,
            out_specs=(vm,) * 4,
            scratch_shapes=[
                pltpu.VMEM((mine, half, toks), BF16),
                pltpu.VMEM((mine, half, toks), BF16),
                square, square, square, square,
                by_tok, by_tok,
                pltpu.VMEM((mine, toks, toks), F32),
                by_tok,
                pltpu.VMEM((mine, half, toks), F32),
                pltpu.VMEM((2, 8, toks), F32),
                dma((2,)), dma((2,)),
                dma((mine,)), dma((mine,)),
                dma((mine,)), dma((mine,)),
                dma((4, mine)), dma((4, mine)),
            ],
            compiler_params=pltpu.CompilerParams(
                collective_id=0, has_side_effects=True, vmem_limit_bytes=32 * 2**20
            ),
        )(query, key, value, beta, d_out)

    rows = P("head", ("groups", "seq"), None)
    cols = P("head", "sub", ("groups", "seq"))
    flat = P("head", ("groups", "seq"))
    return jax.shard_map(
        shards,
        mesh=mesh,
        in_specs=(rows, rows, cols, flat, cols),
        out_specs=(rows, rows, cols, flat),
        check_vma=False,
    )
```

time: 160 us -> 29 us (0.18)
  matrix products: 49.3 us -> 0 us
  blocking collectives: 28.1 us -> 0 us
  waiting for transfers between devices: 26.7 us -> 0 us
  Pallas kernels: 0 us -> 21.3 us
  local copies, waits for them, and re-layouts: 24.3 us -> 6.8 us
  between operations: 14.9 us -> 0.65 us
  starting transfers between devices: 11.1 us -> 0 us
  other arithmetic: 3.1 us -> 0 us
    dot_general x88 -> x0, matrix products: 49.3 us -> none  [the longest x15 8.18 us: block_prep(): jnp.einsum('hncd,hnde->hnce', nil_power, nil_power, precision=HIGH)]
    all_gather x1 -> x0, blocking collectives: 25.1 us -> none  [carried_in(): everything = jax.tree.map(lambda part: lax.all_gather(part, axis), value)]
    pallas_call x0 -> x1, Pallas kernels: none -> 21.3 us  [shards(): pl.pallas_call(functools.partial(kernel, n), out_shape=(jax.ShapeDtypeStr...]
    psum x1 -> x0, waiting for transfers between devices: 15.9 us -> none  [shards(): lax.psum((grad_query, grad_key, grad_beta), 'sub')]
    ppermute x3 -> x0, starting transfers between devices: 11 us -> none  [passed_along(): return lax.ppermute(block, axis, route)]
    ppermute x3 -> x0, waiting for transfers between devices: 10.8 us -> none  [passed_along(): return lax.ppermute(block, axis, route)]
    while x39 -> x0, local copies, waits for them, and re-layouts: 6.74 us -> none
    unnamed x86 -> x14, local copies, waits for them, and re-layouts: 12 us -> 6.8 us
  transfers between devices with their start and end apart: 5 -> 0, of which waited for: 4 -> 0; matrix products, arithmetic and copies ran while one was open for 8% -> 0% of each run, Pallas kernels for 0% -> 0%
where the time goes in v1:
time: 29 us; the launch traced here: 28.7 us
  Pallas kernels  21.3 us (73%)
  local copies, waits for them, and re-layouts  6.8 us (23%)
  between operations  0.65 us (2%)
    pallas_call x1, Pallas kernels, shards(): pl.pallas_call(functools.partial(kernel, n), out_shape=(jax.ShapeDtypeStr...  21.3 us
    unnamed x14, local copies, waits for them, and re-layouts  6.8 us

profile of v1, /device:TPU:0, one launch (start us, length us, event | category | flops | bytes accessed | tf_op | source)
XLA Modules:
  0.0 28.7 jit_solution(9856685355637535883)
XLA Ops:
  0.6 0.0 copy-start
  0.6 0.9 %copy-done = bf16[4,128,128]{2,1,0:T(8,128)(2,1)S(1)} copy-done((bf16[4,128,128]{2,1,0:T(8,128)(2,1)S(1)}, bf16[4,128,128]{2,1,0:T(8,128)(2,1)}, u32[]{:S(2)}) %copy-start) | copy-done | bytes 131096
  1.5 0.0 copy-start.1
  1.5 0.9 %copy-done.1 = bf16[4,128,128]{2,1,0:T(8,128)(2,1)S(1)} copy-done((bf16[4,128,128]{2,1,0:T(8,128)(2,1)S(1)}, bf16[4,128,128]{2,1,0:T(8,128)(2,1)}, u32[]{:S(2)}) %copy-start.1) | copy-done | bytes 131096
  2.4 0.0 copy-start.2
  2.4 0.8 %copy-done.2 = bf16[4,64,128]{2,1,0:T(8,128)(2,1)S(1)} copy-done((bf16[4,64,128]{2,1,0:T(8,128)(2,1)S(1)}, bf16[4,64,128]{2,1,0:T(8,128)(2,1)}, u32[]{:S(2)}) %copy-start.2) | copy-done | bytes 65560
  3.3 0.0 copy-start.3
  3.3 0.8 %copy-done.3 = bf16[4,64,128]{2,1,0:T(8,128)(2,1)S(1)} copy-done((bf16[4,64,128]{2,1,0:T(8,128)(2,1)S(1)}, bf16[4,64,128]{2,1,0:T(8,128)(2,1)}, u32[]{:S(2)}) %copy-start.3) | copy-done | bytes 65560
  4.1 0.0 copy-start.4
  4.1 0.7 %copy-done.4 = f32[4,128]{1,0:T(4,128)S(1)} copy-done((f32[4,128]{1,0:T(4,128)S(1)}, f32[4,128]{1,0:T(4,128)}, u32[]{:S(2)}) %copy-start.4) | copy-done | bytes 2072
  4.8 21.3 %shard_map.84 = (f32[4,128,128]{2,1,0:T(8,128)S(1)}, f32[4,128,128]{2,1,0:T(8,128)S(1)}, f32[4,64,128]{2,1,0:T(8,128)S(1)}, f32[4,128]{1,0:T(4,128)S(1)}) custom-call(bf16[4,128,128]{2,1,0:T(8,128)(2,1)S(1)} %copy-done, bf16[4,128,128]{2,1,0:T(8,128)(2,1)S(1)} %copy-done.1, bf16[4,64,128]{2,1,0:T(8,128)(2,1)S(1)} %copy-done.2, f32[4,128]{1,0:T(4,128)S(1)} %copy-done.4, ...), custom_call_target="tpu_custom_call" | custom-call | tf_op jit(solution)/shard_map/pallas_call | solution.py:295
  26.1 0.7 %copy.13 = f32[4,128,128]{2,1,0:T(8,128)} copy(f32[4,128,128]{2,1,0:T(8,128)S(1)} %get-tuple-element.8) | data formatting | bytes 524288
  26.8 0.7 %copy.14 = f32[4,128,128]{2,1,0:T(8,128)} copy(f32[4,128,128]{2,1,0:T(8,128)S(1)} %get-tuple-element.9) | data formatting | bytes 524288
  27.5 0.7 %copy.15 = f32[4,64,128]{2,1,0:T(8,128)} copy(f32[4,64,128]{2,1,0:T(8,128)S(1)} %get-tuple-element.10) | data formatting | bytes 262144
  28.2 0.6 %copy.16 = f32[4,128]{1,0:T(4,128)} copy(f32[4,128]{1,0:T(4,128)S(1)} %get-tuple-element.11) | data formatting | bytes 4096
Async XLA Ops:
  0.6 0.9 %copy-start = (bf16[4,128,128]{2,1,0:T(8,128)(2,1)S(1)}, bf16[4,128,128]{2,1,0:T(8,128)(2,1)}, u32[]{:S(2)}) copy-start(bf16[4,128,128]{2,1,0:T(8,128)(2,1)} %q_ref.1) | copy-start | bytes 393220
  1.5 0.9 %copy-start.1 = (bf16[4,128,128]{2,1,0:T(8,128)(2,1)S(1)}, bf16[4,128,128]{2,1,0:T(8,128)(2,1)}, u32[]{:S(2)}) copy-start(bf16[4,128,128]{2,1,0:T(8,128)(2,1)} %k_ref.1) | copy-start | bytes 393220
  2.4 0.8 %copy-start.2 = (bf16[4,64,128]{2,1,0:T(8,128)(2,1)S(1)}, bf16[4,64,128]{2,1,0:T(8,128)(2,1)}, u32[]{:S(2)}) copy-start(bf16[4,64,128]{2,1,0:T(8,128)(2,1)} %v_ref.1) | copy-start | bytes 196612
  3.3 0.8 %copy-start.3 = (bf16[4,64,128]{2,1,0:T(8,128)(2,1)S(1)}, bf16[4,64,128]{2,1,0:T(8,128)(2,1)}, u32[]{:S(2)}) copy-start(bf16[4,64,128]{2,1,0:T(8,128)(2,1)} %g_ref.1) | copy-start | bytes 196612
  4.1 0.7 %copy-start.4 = (f32[4,128]{1,0:T(4,128)S(1)}, f32[4,128]{1,0:T(4,128)}, u32[]{:S(2)}) copy-start(f32[4,128]{1,0:T(4,128)} %b_ref.1) | copy-start | bytes 6148

commit v2 on v1

--- a/solution.py
+++ b/solution.py
@@ -9,6 +9,7 @@
 
 EPS = 1e-06
 BASE = 16
+PIECES = 2
 F32 = jnp.float32
 BF16 = jnp.bfloat16
 MESH = pl.DeviceIdType.MESH
@@ -72,8 +73,8 @@
 
 def kernel(
     n, q_ref, k_ref, v_ref, b_ref, g_ref, gq_ref, gk_ref, gv_ref, gb_ref,
-    vin, gin, s_in, s_out, d_in, d_out, dt_s, xt_s, dm_s, gt_s, gvx, gbx,
-    in_send, in_recv, f_send, f_recv, r_send, r_recv, o_send, o_recv,
+    q_own, k_own, b_own, v_own, g_own, s_in, s_out, d_in, d_out, dt_s, xt_s, dm_s, gt_s, gvx, gbx,
+    load, in_send, in_recv, f_send, f_recv, r_send, r_recv, o_send, o_recv,
 ):
     heads, toks, width = q_ref.shape
     mine = heads // 2
@@ -86,6 +87,23 @@
     base = sub * mine
     hs = range(mine)
 
+    own = pl.ds(base, mine)
+    first, second = pl.ds(0, half), pl.ds(half, half)
+    loads = [
+        pltpu.make_async_copy(src, dst, load.at[i])
+        for i, (src, dst) in enumerate(
+            (
+                (k_ref.at[own], k_own),
+                (b_ref, b_own),
+                (q_ref.at[own], q_own),
+                (v_ref.at[own], v_own.at[:, first]),
+                (g_ref.at[own], g_own.at[:, first]),
+            )
+        )
+    ]
+    for copy in loads:
+        copy.start()
+
     barrier = pltpu.get_barrier_semaphore()
     for target in ({"sub": other}, {"seq": right}, {"seq": left}):
         pl.semaphore_signal(barrier, inc=1, device_id=target, device_id_type=MESH)
@@ -97,14 +115,24 @@
         )
 
     away = pl.ds(other * mine, mine)
-    v_copy = remote(v_ref.at[away], vin, in_send.at[0], in_recv.at[0], {"sub": other})
-    g_copy = remote(g_ref.at[away], gin, in_send.at[1], in_recv.at[1], {"sub": other})
-
-    def f_copy(h):
-        return remote(s_out.at[h], s_in.at[h], f_send.at[h], f_recv.at[h], {"seq": right})
-
-    def r_copy(h):
-        return remote(d_out.at[h], d_in.at[h], r_send.at[h], r_recv.at[h], {"seq": left})
+    v_copy = remote(v_ref.at[away], v_own.at[:, second], in_send.at[0], in_recv.at[0], {"sub": other})
+    g_copy = remote(g_ref.at[away], g_own.at[:, second], in_send.at[1], in_recv.at[1], {"sub": other})
+
+    piece = s_in.shape[1] // PIECES
+    cuts = [slice(p * piece, (p + 1) * piece) for p in range(PIECES)]
+    parts = [pl.ds(p * piece, piece) for p in range(PIECES)]
+
+    def f_copy(h, p):
+        return remote(
+            s_out.at[h, parts[p]], s_in.at[h, parts[p]], f_send.at[h, p], f_recv.at[h, p],
+            {"seq": right},
+        )
+
+    def r_copy(h, p):
+        return remote(
+            d_out.at[h, parts[p]], d_in.at[h, parts[p]], r_send.at[h, p], r_recv.at[h, p],
+            {"seq": left},
+        )
 
     def q_copy(h):
         at = gq_ref.at[base + h]
@@ -138,12 +166,13 @@
     below, lower, above = row > col, row >= col, row < col
     eye = (row == col).astype(F32)
 
-    kb = [k_ref[base + h] for h in hs]
-    qb = [q_ref[base + h] for h in hs]
+    loads[0].wait()
+    loads[1].wait()
+    kb = [k_own[h] for h in hs]
     kf = [k.astype(F32) for k in kb]
     r_col = [lax.rsqrt(jnp.sum(k * k, axis=1, keepdims=True) + EPS) for k in kf]
     r_row = [jnp.broadcast_to(r, (toks, toks)).T for r in r_col]
-    b_row = [b_ref[pl.ds(base + h, 1), :] for h in hs]
+    b_row = [b_own[pl.ds(base + h, 1), :] for h in hs]
     b_col = [jnp.broadcast_to(b, (toks, toks)).T for b in b_row]
     both = [nt([kb[h]], [kb[h]]) * r_col[h] * r_row[h] for h in hs]
     tri = inverses([jnp.where(below, b_col[h] * both[h], 0.0) for h in hs], row, col)
@@ -154,10 +183,13 @@
     trans = [split(eye - nn(list(split(w_t[h] * r_row[h])), [kb[h]] * 2)) for h in hs]
     w_s = [split(w) for w in w_t]
 
+    for copy in loads[2:]:
+        copy.wait()
     v_copy.wait_recv()
     g_copy.wait_recv()
-    vt = [jnp.concatenate([v_ref[base + h], vin[h]], axis=0) for h in hs]
-    gt = [jnp.concatenate([g_ref[base + h], gin[h]], axis=0) for h in hs]
+    qb = [q_own[h] for h in hs]
+    vt = [v_own[h] for h in hs]
+    gt = [g_own[h] for h in hs]
     u_t = [nt([vt[h]] * 2, list(tri_b[h])) for h in hs]
     carry = [nn(list(split(u_t[h] * r_row[h])), [kb[h]] * 2) for h in hs]
 
@@ -165,7 +197,8 @@
     def _():
         for h in hs:
             s_out[h] = carry[h]
-            f_copy(h).start()
+            for p in range(PIECES):
+                f_copy(h, p).start()
 
     scores = [
         split(jnp.where(lower, nt([qb[h]], [kb[h]]) * (r_row[h] * scale), 0.0)) for h in hs
@@ -183,62 +216,57 @@
     def _():
         for h in hs:
             d_out[h] = back[h]
-            r_copy(h).start()
+            for p in range(PIECES):
+                r_copy(h, p).start()
 
     z_t = [
         split(nn([kbt[h]] * 2, list(split(tri[h] * r_col[h])))) for h in hs
     ]
     g_tok = [g.T for g in gt]
 
-    def phase_f():
-        for h in hs:
+    def phase_f(h):
+        for p in range(PIECES):
 
             @pl.when(idx > 0)
             def _():
-                f_copy(h).wait_recv()
+                f_copy(h, p).wait_recv()
 
             @pl.when((idx > 0) & (idx < n - 1))
             def _():
-                s_out[h] = nn3(split(s_in[h]), trans[h]) + carry[h]
-                f_copy(h).start()
-
-        for h in hs:
-            state = split(s_in[h])
-            d_t = u_t[h] - nn3(state, w_s[h])
-            xt_s[h] = vt[h].astype(F32) - nt(list(state), [kb[h]] * 2) * r_row[h]
-            dt_s[h] = d_t
-            dm = jnp.where(lower, nn([g_tok[h]] * 2, list(split(d_t))), 0.0)
-            dm_s[h] = dm.T * scale
-            gq_ref[base + h] = scale * nn(
-                [g_tok[h]] * 2 + list(split(dm * r_row[h])), list(state) + [kb[h]] * 2
-            )
-            q_copy(h).start()
-
-    def phase_r():
-        for h in hs:
+                s_out[h, cuts[p]] = nn3(split(s_in[h, cuts[p]]), trans[h]) + carry[h][cuts[p]]
+                f_copy(h, p).start()
+
+        state = split(s_in[h])
+        d_t = u_t[h] - nn3(state, w_s[h])
+        xt_s[h] = vt[h].astype(F32) - nt(list(state), [kb[h]] * 2) * r_row[h]
+        dt_s[h] = d_t
+        dm = jnp.where(lower, nn([g_tok[h]] * 2, list(split(d_t))), 0.0)
+        dm_s[h] = dm.T * scale
+        gq_ref[base + h] = scale * nn(
+            [g_tok[h]] * 2 + list(split(dm * r_row[h])), list(state) + [kb[h]] * 2
+        )
+        q_copy(h).start()
+
+    def phase_r(h):
+        for p in range(PIECES):
 
             @pl.when(idx < n - 1)
             def _():
-                r_copy(h).wait_recv()
+                r_copy(h, p).wait_recv()
 
             @pl.when((idx > 0) & (idx < n - 1))
             def _():
-                d_out[h] = nt3(split(d_in[h]), trans[h]) + back[h]
-                r_copy(h).start()
-
-        for h in hs:
-            g_full = g0[h] + nn3(split(d_in[h]), z_t[h])
-            gt_s[h] = g_full
-            e_t = g_full * b_row[h]
-            gv_ref[base + h] = e_t[:half]
-            gvx[h] = e_t[half:]
-            gv_copy(h).start()
-
-    pl.when(2 * idx < n)(phase_f)
-    phase_r()
-    pl.when(2 * idx >= n)(phase_f)
-
-    for h in hs:
+                d_out[h, cuts[p]] = nt3(split(d_in[h, cuts[p]]), trans[h]) + back[h][cuts[p]]
+                r_copy(h, p).start()
+
+        g_full = g0[h] + nn3(split(d_in[h]), z_t[h])
+        gt_s[h] = g_full
+        e_t = g_full * b_row[h]
+        gv_ref[base + h] = e_t[:half]
+        gvx[h] = e_t[half:]
+        gv_copy(h).start()
+
+    def finish(h):
         g_full, d_t = gt_s[h], dt_s[h]
         d_tok = split(d_t.T)
         e_tok = split(-(g_full * b_row[h]).T)
@@ -257,6 +285,23 @@
             d_unit - unit * jnp.sum(d_unit * unit, axis=1, keepdims=True)
         )
         k_copy(h).start()
+
+    @pl.when(2 * idx < n)
+    def _():
+        for h in hs:
+            phase_f(h)
+        for h in hs:
+            phase_r(h)
+            finish(h)
+
+    @pl.when(2 * idx >= n)
+    def _():
+        for h in hs:
+            phase_r(h)
+        for h in hs:
+            phase_f(h)
+            finish(h)
+
     gb_copy.start()
 
     v_copy.wait_send()
@@ -265,12 +310,14 @@
     @pl.when(idx < n - 1)
     def _():
         for h in hs:
-            f_copy(h).wait_send()
+            for p in range(PIECES):
+                f_copy(h, p).wait_send()
 
     @pl.when(idx > 0)
     def _():
         for h in hs:
-            r_copy(h).wait_send()
+            for p in range(PIECES):
+                r_copy(h, p).wait_send()
 
     for h in hs:
         q_copy(h).wait()
@@ -281,6 +328,15 @@
         gb_ref[s * mine : (s + 1) * mine, :] = gbx[s, :mine, :]
 
 
+def write_out(*refs):
+    sems = refs[-1]
+    copies = [pltpu.make_async_copy(refs[i], refs[4 + i], sems.at[i]) for i in range(4)]
+    for copy in copies:
+        copy.start()
+    for copy in copies:
+        copy.wait()
+
+
 def solution(mesh):
     n = mesh.shape["seq"]
 
@@ -289,37 +345,49 @@
         mine, half = heads // 2, value.shape[1]
         full = 2 * half
         vm = pl.BlockSpec(memory_space=pltpu.VMEM)
+        hbm = pl.BlockSpec(memory_space=pltpu.HBM)
         dma = pltpu.SemaphoreType.DMA
         square = pltpu.VMEM((mine, full, width), F32)
         by_tok = pltpu.VMEM((mine, full, toks), F32)
-        return pl.pallas_call(
+        pinned = [pltpu.with_memory_space_constraint(x, pltpu.HBM) for x in (query, key, value, beta, d_out)]
+        found = pl.pallas_call(
             functools.partial(kernel, n),
             out_shape=(
-                jax.ShapeDtypeStruct(query.shape, F32),
-                jax.ShapeDtypeStruct(key.shape, F32),
-                jax.ShapeDtypeStruct(value.shape, F32),
-                jax.ShapeDtypeStruct(beta.shape, F32),
+                pltpu.VMEM(query.shape, F32),
+                pltpu.VMEM(key.shape, F32),
+                pltpu.VMEM(value.shape, F32),
+                pltpu.VMEM(beta.shape, F32),
             ),
-            in_specs=[vm] * 5,
+            in_specs=[hbm] * 5,
             out_specs=(vm,) * 4,
             scratch_shapes=[
-                pltpu.VMEM((mine, half, toks), BF16),
-                pltpu.VMEM((mine, half, toks), BF16),
+                pltpu.VMEM((mine, toks, width), BF16),
+                pltpu.VMEM((mine, toks, width), BF16),
+                pltpu.VMEM((heads, toks), F32),
+                pltpu.VMEM((mine, full, toks), BF16),
+                pltpu.VMEM((mine, full, toks), BF16),
                 square, square, square, square,
                 by_tok, by_tok,
                 pltpu.VMEM((mine, toks, toks), F32),
                 by_tok,
                 pltpu.VMEM((mine, half, toks), F32),
                 pltpu.VMEM((2, 8, toks), F32),
-                dma((2,)), dma((2,)),
-                dma((mine,)), dma((mine,)),
-                dma((mine,)), dma((mine,)),
+                dma((5,)), dma((2,)), dma((2,)),
+                dma((mine, PIECES)), dma((mine, PIECES)),
+                dma((mine, PIECES)), dma((mine, PIECES)),
                 dma((4, mine)), dma((4, mine)),
             ],
             compiler_params=pltpu.CompilerParams(
                 collective_id=0, has_side_effects=True, vmem_limit_bytes=32 * 2**20
             ),
-        )(query, key, value, beta, d_out)
+        )(*pinned)
+        return pl.pallas_call(
+            write_out,
+            out_shape=tuple(jax.ShapeDtypeStruct(x.shape, F32) for x in found),
+            in_specs=[vm] * 4,
+            out_specs=(hbm,) * 4,
+            scratch_shapes=[dma((4,))],
+        )(*[pltpu.with_memory_space_constraint(x, pltpu.VMEM) for x in found])
 
     rows = P("head", ("groups", "seq"), None)
     cols = P("head", "sub", ("groups", "seq"))

time: 29 us -> 22 us (0.76)
  local copies, waits for them, and re-layouts: 6.8 us -> 0 us
    unnamed x14 -> x0, local copies, waits for them, and re-layouts: 6.8 us -> none
    pallas_call x1 -> x2, Pallas kernels: 21.3 us -> 21.3 us  [the longest x1 20.4 us: shards(): pl.pallas_call(functools.partial(kernel, n), out_shape=(pltpu.VMEM(query....]
where the time goes in v2:
time: 22 us; the launch traced here: 21.9 us
  Pallas kernels  21.3 us (97%)
  between operations  0.64 us (3%)
    pallas_call x1, Pallas kernels, shards(): pl.pallas_call(functools.partial(kernel, n), out_shape=(pltpu.VMEM(query....  20.4 us
    pallas_call x1, Pallas kernels, shards(): pl.pallas_call(write_out, out_shape=tuple((jax.ShapeDtypeStruct(x.shape,...  0.87 us

profile of v2, /device:TPU:0, one launch (start us, length us, event | category | flops | bytes accessed | tf_op | source)
XLA Modules:
  0.0 21.9 jit_solution(1764046960719494002)
XLA Ops:
  0.6 20.4 %shard_map.84 = (f32[4,128,128]{2,1,0:T(8,128)S(1)}, f32[4,128,128]{2,1,0:T(8,128)S(1)}, f32[4,64,128]{2,1,0:T(8,128)S(1)}, f32[4,128]{1,0:T(4,128)S(1)}) custom-call(bf16[4,128,128]{2,1,0:T(8,128)(2,1)} %q_ref.1, bf16[4,128,128]{2,1,0:T(8,128)(2,1)} %k_ref.1, bf16[4,64,128]{2,1,0:T(8,128)(2,1)} %v_ref.1, f32[4,128]{1,0:T(4,128)} %b_ref.1, ...), custom_call_target="tpu_custom_call" | custom-call | tf_op jit(solution)/shard_map/pallas_call | solution.py:353
  21.0 0.9 %shard_map.85 = (f32[4,128,128]{2,1,0:T(8,128)}, f32[4,128,128]{2,1,0:T(8,128)}, f32[4,64,128]{2,1,0:T(8,128)}, f32[4,128]{1,0:T(4,128)}) custom-call(f32[4,128,128]{2,1,0:T(8,128)S(1)} %get-tuple-element.8.refs_0_, f32[4,128,128]{2,1,0:T(8,128)S(1)} %get-tuple-element.9.refs_1_, f32[4,64,128]{2,1,0:T(8,128)S(1)} %get-tuple-element.10.refs_2_, ...), custom_call_target="tpu_custom_call" | custom-call | tf_op jit(solution)/shard_map/pallas_call | solution.py:384

commit v3 on v2

--- a/solution.py
+++ b/solution.py
@@ -8,7 +8,7 @@
 from jax.sharding import PartitionSpec as P
 
 EPS = 1e-06
-BASE = 16
+BASE = 32
 PIECES = 2
 F32 = jnp.float32
 BF16 = jnp.bfloat16
@@ -224,17 +224,31 @@
     ]
     g_tok = [g.T for g in gt]
 
+    inside = (idx > 0) & (idx < n - 1)
+
+    def relay_f():
+        @pl.when(inside)
+        def _():
+            for h in hs:
+                for p in range(PIECES):
+                    f_copy(h, p).wait_recv()
+                    s_out[h, cuts[p]] = nn3(split(s_in[h, cuts[p]]), trans[h]) + carry[h][cuts[p]]
+                    f_copy(h, p).start()
+
+    def relay_r():
+        @pl.when(inside)
+        def _():
+            for h in hs:
+                for p in range(PIECES):
+                    r_copy(h, p).wait_recv()
+                    d_out[h, cuts[p]] = nt3(split(d_in[h, cuts[p]]), trans[h]) + back[h][cuts[p]]
+                    r_copy(h, p).start()
+
     def phase_f(h):
-        for p in range(PIECES):
-
-            @pl.when(idx > 0)
-            def _():
+        @pl.when(idx == n - 1)
+        def _():
+            for p in range(PIECES):
                 f_copy(h, p).wait_recv()
-
-            @pl.when((idx > 0) & (idx < n - 1))
-            def _():
-                s_out[h, cuts[p]] = nn3(split(s_in[h, cuts[p]]), trans[h]) + carry[h][cuts[p]]
-                f_copy(h, p).start()
 
         state = split(s_in[h])
         d_t = u_t[h] - nn3(state, w_s[h])
@@ -248,16 +262,10 @@
         q_copy(h).start()
 
     def phase_r(h):
-        for p in range(PIECES):
-
-            @pl.when(idx < n - 1)
-            def _():
+        @pl.when(idx == 0)
+        def _():
+            for p in range(PIECES):
                 r_copy(h, p).wait_recv()
-
-            @pl.when((idx > 0) & (idx < n - 1))
-            def _():
-                d_out[h, cuts[p]] = nt3(split(d_in[h, cuts[p]]), trans[h]) + back[h][cuts[p]]
-                r_copy(h, p).start()
 
         g_full = g0[h] + nn3(split(d_in[h]), z_t[h])
         gt_s[h] = g_full
@@ -288,16 +296,20 @@
 
     @pl.when(2 * idx < n)
     def _():
+        relay_f()
         for h in hs:
             phase_f(h)
+        relay_r()
         for h in hs:
             phase_r(h)
             finish(h)
 
     @pl.when(2 * idx >= n)
     def _():
+        relay_r()
         for h in hs:
             phase_r(h)
+        relay_f()
         for h in hs:
             phase_f(h)
             finish(h)

time: 22 us -> 21.4 us (0.973)
  Pallas kernels: 21.3 us -> 20.6 us
    pallas_call x1, Pallas kernels: 20.4 us -> 19.8 us  [shards(): pl.pallas_call(functools.partial(kernel, n), out_shape=(pltpu.VMEM(query....]
where the time goes in v3:
time: 21.4 us; the launch traced here: 21.3 us
  Pallas kernels  20.6 us (96%)
  between operations  0.64 us (3%)
    pallas_call x1, Pallas kernels, shards(): pl.pallas_call(functools.partial(kernel, n), out_shape=(pltpu.VMEM(query....  19.8 us
    pallas_call x1, Pallas kernels, shards(): pl.pallas_call(write_out, out_shape=tuple((jax.ShapeDtypeStruct(x.shape,...  0.87 us

profile of v3, /device:TPU:0, one launch (start us, length us, event | category | flops | bytes accessed | tf_op | source)
XLA Modules:
  0.0 21.3 jit_solution(11513499883418510827)
XLA Ops:
  0.6 19.8 %shard_map.84 = (f32[4,128,128]{2,1,0:T(8,128)S(1)}, f32[4,128,128]{2,1,0:T(8,128)S(1)}, f32[4,64,128]{2,1,0:T(8,128)S(1)}, f32[4,128]{1,0:T(4,128)S(1)}) custom-call(bf16[4,128,128]{2,1,0:T(8,128)(2,1)} %q_ref.1, bf16[4,128,128]{2,1,0:T(8,128)(2,1)} %k_ref.1, bf16[4,64,128]{2,1,0:T(8,128)(2,1)} %v_ref.1, f32[4,128]{1,0:T(4,128)} %b_ref.1, ...), custom_call_target="tpu_custom_call" | custom-call | tf_op jit(solution)/shard_map/pallas_call | solution.py:365
  20.4 0.9 %shard_map.85 = (f32[4,128,128]{2,1,0:T(8,128)}, f32[4,128,128]{2,1,0:T(8,128)}, f32[4,64,128]{2,1,0:T(8,128)}, f32[4,128]{1,0:T(4,128)}) custom-call(f32[4,128,128]{2,1,0:T(8,128)S(1)} %get-tuple-element.8.refs_0_, f32[4,128,128]{2,1,0:T(8,128)S(1)} %get-tuple-element.9.refs_1_, f32[4,64,128]{2,1,0:T(8,128)S(1)} %get-tuple-element.10.refs_2_, ...), custom_call_target="tpu_custom_call" | custom-call | tf_op jit(solution)/shard_map/pallas_call | solution.py:396

commit v4 on v3

--- a/solution.py
+++ b/solution.py
@@ -105,8 +105,20 @@
         copy.start()
 
     barrier = pltpu.get_barrier_semaphore()
-    for target in ({"sub": other}, {"seq": right}, {"seq": left}):
+    inside = (idx > 0) & (idx < n - 1)
+
+    def greet(target):
         pl.semaphore_signal(barrier, inc=1, device_id=target, device_id_type=MESH)
+
+    greet({"sub": other})
+
+    @pl.when(idx < n - 1)
+    def _():
+        greet({"seq": right})
+
+    @pl.when(idx > 0)
+    def _():
+        greet({"seq": left})
 
     def remote(src, dst, send, recv, target):
         return pltpu.make_async_remote_copy(
@@ -149,7 +161,14 @@
 
     gb_copy = remote(gbx.at[sub], gbx.at[sub], o_send.at[3, 0], o_recv.at[3, 0], {"sub": other})
 
-    pl.semaphore_wait(barrier, 3)
+    @pl.when(inside)
+    def _():
+        pl.semaphore_wait(barrier, 3)
+
+    @pl.when(jnp.logical_not(inside))
+    def _():
+        pl.semaphore_wait(barrier, 2)
+
     v_copy.start()
     g_copy.start()
 
@@ -223,8 +242,6 @@
         split(nn([kbt[h]] * 2, list(split(tri[h] * r_col[h])))) for h in hs
     ]
     g_tok = [g.T for g in gt]
-
-    inside = (idx > 0) & (idx < n - 1)
 
     def relay_f():
         @pl.when(inside)

time: 21.4 us -> 21.4 us (level)
  no operation moved by 1% of the time
where the time goes in v4:
time: 21.4 us; the launch traced here: 21.3 us
  Pallas kernels  20.6 us (96%)
  between operations  0.64 us (3%)
    pallas_call x1, Pallas kernels, shards(): pl.pallas_call(functools.partial(kernel, n), out_shape=(pltpu.VMEM(query....  19.8 us
    pallas_call x1, Pallas kernels, shards(): pl.pallas_call(write_out, out_shape=tuple((jax.ShapeDtypeStruct(x.shape,...  0.87 us

profile of v4, /device:TPU:0, one launch (start us, length us, event | category | flops | bytes accessed | tf_op | source)
XLA Modules:
  0.0 21.3 jit_solution(16324378879522485433)
XLA Ops:
  0.6 19.8 %shard_map.84 = (f32[4,128,128]{2,1,0:T(8,128)S(1)}, f32[4,128,128]{2,1,0:T(8,128)S(1)}, f32[4,64,128]{2,1,0:T(8,128)S(1)}, f32[4,128]{1,0:T(4,128)S(1)}) custom-call(bf16[4,128,128]{2,1,0:T(8,128)(2,1)} %q_ref.1, bf16[4,128,128]{2,1,0:T(8,128)(2,1)} %k_ref.1, bf16[4,64,128]{2,1,0:T(8,128)(2,1)} %v_ref.1, f32[4,128]{1,0:T(4,128)} %b_ref.1, ...), custom_call_target="tpu_custom_call" | custom-call | tf_op jit(solution)/shard_map/pallas_call | solution.py:382
  20.4 0.9 %shard_map.85 = (f32[4,128,128]{2,1,0:T(8,128)}, f32[4,128,128]{2,1,0:T(8,128)}, f32[4,64,128]{2,1,0:T(8,128)}, f32[4,128]{1,0:T(4,128)}) custom-call(f32[4,128,128]{2,1,0:T(8,128)S(1)} %get-tuple-element.8.refs_0_, f32[4,128,128]{2,1,0:T(8,128)S(1)} %get-tuple-element.9.refs_1_, f32[4,64,128]{2,1,0:T(8,128)S(1)} %get-tuple-element.10.refs_2_, ...), custom_call_target="tpu_custom_call" | custom-call | tf_op jit(solution)/shard_map/pallas_call | solution.py:413
